TPU v7x, 32 devices: a whole 2x2x4 slice. The times are simulated.
32 devices in a mesh: seq: 8 (over z, y), tensor: 4 (over x, core).
Axes of the slice: x: 2, y: 2, z: 4, core: 2. Of those that a mesh axis runs over, the one named last changes fastest.
Arguments:
- stream: bfloat16 [32, 2304], P('seq'), may hold values from -6 to 6
- new_query: bfloat16 [32, 2304], P('seq', 'tensor'), may hold values from -13 to 13
- k_new: bfloat16 [32, 2304], P('seq', 'tensor'), may hold values from -5 to 5
- v_new: bfloat16 [32, 2304], P('seq', 'tensor'), may hold values from -5 to 5
- k_cache: bfloat16 [32, 64, 2304], P('seq', None, 'tensor'), may hold values from -4 to 4
- v_cache: bfloat16 [32, 64, 2304], P('seq', None, 'tensor'), may hold values from -5 to 5
- page_owner: int32 [32], replicated, may hold values from 0 to 31
- page_fill: int32 [32], P('seq'), may hold values from 2 to 64
- out_weight: bfloat16 [2304, 2304], P('tensor', 'seq'), may hold values from -0.125 to 0.125
- norm_gain: float32 [2304], replicated, may hold values from 0.5 to 1.5
- routes: int32 [32, 2], P('seq'), may hold values from 0 to 7, all different within a row; in each aligned block of 4 rows (0 to 3, 4 to 7, ...) at most 2 rows name the same one
- route_weight: float32 [32, 2], P('seq'), may hold values from 0.2 to 1
- w_gate: bfloat16 [8, 2304, 5760], P('seq', 'tensor'), may hold values from -0.125 to 0.125
- w_up: bfloat16 [8, 2304, 5760], P('seq', 'tensor'), may hold values from -0.125 to 0.125
- w_down: bfloat16 [8, 5760, 2304], P('seq', None, 'tensor'), may hold values from -0.078125 to 0.078125
Outputs:
- attn_out: bfloat16 [32, 2304], P('seq', 'tensor')
- moe_out: bfloat16 [32, 2304], P('seq', 'tensor')
Inputs may be any that keep to these rules, and one draw needn't show every extreme that they name: `routes`: each request names 2 different experts; among the 4 requests of one index of seq (an aligned block) no expert is named more than 2 times, and in some blocks one is named exactly 2 times.
All inputs are finite; a program needn't handle non-finite values.
Results may differ from a plain program's by a relative error of at most 0.012.
Values may be sent and summed in bfloat16 or wider, within the bound.
A program may use at most 64 MiB of HBM per device.

v0:
```python
import math

import jax
import jax.numpy as jnp
from jax import lax
from jax.sharding import PartitionSpec as P

HEAD_DIM = 64
EXPERTS = 8
CAP = 2


low_value = -1e30
eps = 1e-05


def per_device(
    stream,
    new_query,
    k_new,
    v_new,
    k_cache,
    v_cache,
    page_owner,
    page_fill,
    out_weight,
    norm_gain,
    routes,
    route_weight,
    w_gate,
    w_up,
    w_down,
):
    seq_count = lax.axis_size("seq")
    seq_rank = lax.axis_index("seq")
    tensor_rank = lax.axis_index("tensor")
    req_dev = stream.shape[0]
    requests = req_dev * seq_count
    width = new_query.shape[1]
    heads_dev = width // HEAD_DIM
    pages_dev = k_cache.shape[0]
    page_len = k_cache.shape[1]
    model_width = stream.shape[1]
    quarter = model_width // lax.axis_size("tensor")
    scale = 1.0 / math.sqrt(HEAD_DIM)
    local_owner = lax.dynamic_slice_in_dim(page_owner, seq_rank * pages_dev, pages_dev, 0)
    all_queries = lax.all_gather(new_query, "seq", axis=0, tiled=True)
    page_queries = jnp.take(all_queries, local_owner, axis=0).reshape(
        pages_dev, heads_dev, HEAD_DIM
    )
    keys = k_cache.reshape(pages_dev, page_len, heads_dev, HEAD_DIM)
    values = v_cache.reshape(pages_dev, page_len, heads_dev, HEAD_DIM).astype(jnp.float32)
    scores = (
        jnp.einsum("phd,pjhd->phj", page_queries, keys, preferred_element_type=jnp.float32) * scale
    )
    valid = lax.broadcasted_iota(jnp.int32, (pages_dev, page_len), 1) < page_fill[:, None]
    scores = jnp.where(valid[:, None, :], scores, low_value)
    page_top = jnp.max(scores, axis=2)
    weights = jnp.exp(scores - page_top[:, :, None])
    page_sum = jnp.sum(weights, axis=2)
    page_acc = jnp.einsum("phj,pjhd->phd", weights, values, precision=lax.Precision.HIGHEST)
    resident_query_rows = new_query.reshape(req_dev, heads_dev, HEAD_DIM)
    own_keys = k_new.reshape(req_dev, heads_dev, HEAD_DIM)
    own_score = (
        jnp.einsum("rhd,rhd->rh", resident_query_rows, own_keys, preferred_element_type=jnp.float32)
        * scale
    )
    own_values = v_new.reshape(req_dev, heads_dev, HEAD_DIM).astype(jnp.float32)
    home_start = seq_rank * req_dev
    request_ids = lax.broadcasted_iota(jnp.int32, (pages_dev, requests), 1)
    owner_hot = local_owner[:, None] == request_ids
    dense_top = jnp.max(jnp.where(owner_hot[:, :, None], page_top[:, None, :], low_value), axis=0)
    local_top_maximum = jnp.maximum(
        lax.dynamic_slice_in_dim(dense_top, home_start, req_dev, 0), own_score
    )
    dense_top = lax.dynamic_update_slice_in_dim(dense_top, local_top_maximum, home_start, 0)
    global_top = lax.pmax(dense_top, "seq")
    factor = jnp.exp(page_top - jnp.take(global_top, local_owner, axis=0))
    hot = owner_hot.astype(jnp.float32)
    dense_sum = jnp.einsum("pr,ph->rh", hot, page_sum * factor, precision=lax.Precision.HIGHEST)
    dense_acc = jnp.einsum(
        "pr,phd->rhd", hot, page_acc * factor[:, :, None], precision=lax.Precision.HIGHEST
    )
    own_factor = jnp.exp(own_score - lax.dynamic_slice_in_dim(global_top, home_start, req_dev, 0))
    home_sum = lax.dynamic_slice_in_dim(dense_sum, home_start, req_dev, 0) + own_factor
    dense_sum = lax.dynamic_update_slice_in_dim(dense_sum, home_sum, home_start, 0)
    home_acc = (
        lax.dynamic_slice_in_dim(dense_acc, home_start, req_dev, 0)
        + own_factor[:, :, None] * own_values
    )
    dense_acc = lax.dynamic_update_slice_in_dim(dense_acc, home_acc, home_start, 0)
    merged_sum, merged_acc = lax.psum((dense_sum, dense_acc), "seq")
    attention = merged_acc / merged_sum[:, :, None]
    attended = attention.reshape(requests, width).astype(jnp.bfloat16)
    projected_part = jnp.dot(attended, out_weight, preferred_element_type=jnp.float32)
    home_part = lax.all_to_all(projected_part, "seq", split_axis=0, concat_axis=1, tiled=True)
    attn_full = lax.psum(home_part, "tensor")
    attention_rounded = attn_full.astype(jnp.bfloat16)
    attn_out = lax.dynamic_slice_in_dim(attention_rounded, tensor_rank * quarter, quarter, 1)
    resid = stream.astype(jnp.float32) + attention_rounded.astype(jnp.float32)
    normed = resid * lax.rsqrt(jnp.mean(resid * resid, axis=-1, keepdims=True) + eps) * norm_gain
    normed = normed.astype(jnp.bfloat16)
    my_columns = lax.dynamic_slice_in_dim(normed, tensor_rank * quarter, quarter, 1)
    expert_ids = lax.broadcasted_iota(jnp.int32, (req_dev, EXPERTS), 1)
    chosen = jnp.zeros((req_dev, EXPERTS), jnp.int32)
    coef = jnp.zeros((req_dev, EXPERTS), jnp.float32)
    for route in range(routes.shape[1]):
        match = routes[:, route : route + 1] == expert_ids
        chosen = chosen + match.astype(jnp.int32)
        coef = coef + jnp.where(match, route_weight[:, route : route + 1], 0.0)
    rank = jnp.cumsum(chosen, axis=0) - chosen
    slot_ids = lax.broadcasted_iota(jnp.int32, (EXPERTS, CAP, req_dev), 1)
    placed = (chosen.T[:, None, :] == 1) & (rank.T[:, None, :] == slot_ids)
    slices = seq_count // EXPERTS
    placed_dest = jnp.repeat(placed, slices, axis=0)
    send = jnp.einsum(
        "lwb,bo->lwo",
        placed_dest.astype(jnp.bfloat16),
        my_columns,
        preferred_element_type=jnp.float32,
    ).astype(jnp.bfloat16)
    rows = lax.all_to_all(send, "seq", split_axis=0, concat_axis=0, tiled=True)
    count_src, count_items, columns = rows.shape
    flat = rows.reshape(count_src * count_items, columns)
    gate_part = jnp.dot(flat, w_gate[0], preferred_element_type=jnp.float32)
    up_part = jnp.dot(flat, w_up[0], preferred_element_type=jnp.float32)
    stacked = jnp.stack([gate_part, up_part])
    summed = lax.psum(stacked, "tensor")
    hidden = (jax.nn.silu(summed[0]) * summed[1]).astype(jnp.bfloat16)
    down = jnp.dot(hidden, w_down[0], preferred_element_type=jnp.float32)
    expert_out = down.reshape(count_src, count_items, down.shape[1])
    returned_output = lax.all_to_all(
        expert_out.astype(jnp.bfloat16), "seq", split_axis=0, concat_axis=0, tiled=True
    ).astype(expert_out.dtype)
    weighted_output_rows = (
        placed_dest.astype(jnp.float32) * jnp.repeat(coef.T, slices, axis=0)[:, None, :]
    )
    mixture_expert_partial = jnp.einsum(
        "ubp,ubr->pr", weighted_output_rows, returned_output, precision=lax.Precision.HIGHEST
    )
    return (attn_out, mixture_expert_partial.astype(jnp.bfloat16))


def solution(mesh):
    in_specs = (
        P("seq", None),
        P("seq", "tensor"),
        P("seq", "tensor"),
        P("seq", "tensor"),
        P("seq", None, "tensor"),
        P("seq", None, "tensor"),
        P(),
        P("seq"),
        P("tensor", "seq"),
        P(),
        P("seq", None),
        P("seq", None),
        P("seq", "tensor", None),
        P("seq", "tensor", None),
        P("seq", None, "tensor"),
    )
    out_specs = (P("seq", "tensor"), P("seq", "tensor"))
    return jax.shard_map(
        per_device, mesh=mesh, in_specs=in_specs, out_specs=out_specs, check_vma=False
    )
```

profile of v0, /device:TPU:0, one launch (start us, length us, event | category | flops | bytes accessed | tf_op | source)
XLA Modules:
  0.0 238.0 jit_solution(13612010175156103447)
XLA Ops:
  7.2 1.3 copy.40
  8.5 32.6 %all-gather = bf16[8,4,576]{2,1,0:T(4,128)(2,1)S(1)} all-gather(bf16[1,4,576]{2,1,0:T(4,128)(2,1)} %bitcast.70), channel_id=1, replica_groups=mesh['seq'=8,'tensor'=4] {'seq'}, dimensions={0}, use_global_device_ids=true | all-gather | bytes 41472 | tf_op jit(solution)/shard_map/all_gather | solution.py:47
  41.2 0.7 compare_and_fusion
  42.6 0.7 iota_compare_fusion.5
  44.1 0.8 reshape.209
  44.8 1.3 copy.41
  46.2 0.8 reshape.210
  47.4 21.5 %pmax.7 = f32[32,9]{0,1:T(8,128)S(1)} all-reduce(f32[32,9]{0,1:T(8,128)S(1)} %dynamic_update_slice.9), channel_id=1, replica_groups=mesh['seq'=8,'tensor'=4] {'seq'}, use_global_device_ids=true, to_apply=%region_2.3 | all-reduce | flops 288 | bytes 2304 | tf_op jit(solution)/shard_map/pmax | solution.py:77
  69.7 0.8 reshape.212
  70.9 1.0 fusion.17
  72.4 0.6 copy-done.1
  73.1 0.8 slice_bitcast_fusion.3
  74.2 17.6 %psum.29 = f32[32,9]{0,1:T(8,128)S(1)} all-reduce(f32[32,9]{0,1:T(8,128)S(1)} %dynamic_update_slice.11), channel_id=1, replica_groups=mesh['seq'=8,'tensor'=4] {'seq'}, use_global_device_ids=true, to_apply=%region_5.6 | all-reduce | flops 288 | bytes 2304 | tf_op jit(solution)/shard_map/psum | solution.py:92
  91.8 48.6 %all-reduce.3.cloned.1.call-done = f32[32,9,64]{2,0,1:T(8,128)} async-done(((f32[32,9,64]{2,0,1:T(8,128)}), f32[32,9,64]{2,0,1:T(8,128)}) %all-reduce.3.cloned.1.call-update) | async-done | bytes 73744 | tf_op jit(solution)/shard_map/psum | solution.py:92
  140.4 1.0 divide_convert_fusion
  141.6 0.9 fusion.9
  142.5 3.7 %all-to-all-start = ((f32[8,4,288]{2,1,0:T(4,128)}), f32[8,4,288]{2,1,0:T(4,128)S(1)}, u32[]{:S(2)}, u32[]{:S(2)}) async-start(f32[8,4,288]{2,1,0:T(4,128)} %fusion.9), calls=%async_computation | async-start | bytes 98304 | tf_op jit(solution)/shard_map/all_to_all | solution.py:96
  146.2 0.8 dynamic-slice
  147.0 5.9 %all-to-all-done = f32[8,4,288]{2,1,0:T(4,128)S(1)} async-done(((f32[8,4,288]{2,1,0:T(4,128)}), f32[8,4,288]{2,1,0:T(4,128)S(1)}, u32[]{:S(2)}, u32[]{:S(2)}) %all-to-all-start) | async-done | bytes 36896 | tf_op jit(solution)/shard_map/all_to_all | solution.py:96
  153.0 10.5 %psum.30 = bf16[4,2304]{1,0:T(4,128)(2,1)S(1)} all-reduce(f32[4,2304]{1,0:T(4,128)S(1)} %all_to_all.20), channel_id=1, replica_groups=mesh['seq'=8,'tensor'=4] {'tensor'}, use_global_device_ids=true, to_apply=%region_6.7 | all-reduce | flops 9216 | bytes 55296 | tf_op jit(solution)/shard_map/psum | solution.py:97
  163.5 0.9 multiply_reduce_fusion
  164.6 9.0 %all_to_all.26 = bf16[8,2,576]{2,1,0:T(2,128)(2,1)S(1)} all-to-all(bf16[8,2,576]{2,1,0:T(2,128)(2,1)S(1)} %copy.51), channel_id=1, replica_groups=mesh['seq'=8,'tensor'=4] {'seq'}, dimensions={0} | all-to-all | bytes 36864 | tf_op jit(solution)/shard_map/all_to_all | solution.py:122
  173.6 4.1 %convolution_bitcast_fusion = f32[1,16,5760]{2,1,0:T(8,128)S(1)} fusion(bf16[16,576]{1,0:T(8,128)(2,1)S(1)} %reshape.211, bf16[1,576,5760]{2,1,0:T(8,128)(2,1)} %param.28), kind=kOutput, calls=%fused_computation.2 | convolution fusion | flops 106168320 | bytes 7022592 | tf_op jit(solution)/shard_map/dot_general | solution.py:126
  177.8 1.1 convolution_bitcast_fusion.1
  178.8 0.9 pad_maximum_fusion
  179.9 31.8 %all-reduce.5.cloned.1.call-done = f32[2,16,5760]{2,1,0:T(8,128)} async-done(((f32[2,16,5760]{2,1,0:T(8,128)}), f32[2,16,5760]{2,1,0:T(8,128)}) %all-reduce.5.cloned.1.call-update) | async-done | bytes 737296 | tf_op jit(solution)/shard_map/psum | solution.py:128
  211.7 1.2 fusion.8
  212.9 4.7 %fusion.4 = bf16[8,2,576]{2,0,1:T(8,128)(2,1)S(1)} fusion(bf16[1,5760,576]{1,2,0:T(8,128)(2,1)} %param.29, bf16[8,2,5760]{2,1,0:T(2,128)(2,1)S(1)} %convert_element_type.82), kind=kOutput, calls=%fused_computation.8 | convolution fusion | flops 106177536 | bytes 6838272 | tf_op jit(solution)/shard_map/dot_general | solution.py:130
  218.3 5.5 %all-to-all-start.2 = ((bf16[8,2,576]{2,1,0:T(2,128)(2,1)}), bf16[8,2,576]{2,1,0:T(2,128)(2,1)S(1)}, u32[]{:S(2)}, u32[]{:S(2)}) async-start(bf16[8,2,576]{2,1,0:T(2,128)(2,1)} %copy.53), calls=%async_computation.2 | async-start | bytes 40960 | tf_op jit(solution)/shard_map/all_to_all | solution.py:132
  223.8 0.7 constant_dynamic-slice_fusion
  224.5 5.9 %all-to-all-done.2 = bf16[8,2,576]{2,1,0:T(2,128)(2,1)S(1)} async-done(((bf16[8,2,576]{2,1,0:T(2,128)(2,1)}), bf16[8,2,576]{2,1,0:T(2,128)(2,1)S(1)}, u32[]{:S(2)}, u32[]{:S(2)}) %all-to-all-start.2) | async-done | bytes 18464 | tf_op jit(solution)/shard_map/all_to_all | solution.py:132
  230.4 0.8 fusion.7
  (56 shorter events, 5.5 us)
Async XLA Ops:
  7.2 134.4 %copy-start = (bf16[576,288]{0,1:T(8,128)(2,1)S(1)}, bf16[576,288]{0,1:T(8,128)(2,1)}, u32[]{:S(2)}) copy-start(bf16[576,288]{0,1:T(8,128)(2,1)} %param.23) | copy-start | bytes 995332
  7.2 133.2 %all-reduce.3.cloned.1.call-start = ((), (), s32[]{:S(2)}) async-start(), calls=%async_computation.3 | async-start | bytes 294912 | tf_op jit(solution)/shard_map/psum | solution.py:92
  72.4 0.7 copy-start.1
  141.6 36.2 %slice-start = ((s8[6635520]{0:T(1024)(128)(4,1)}), s8[2441216]{0:T(1024)(128)(4,1)S(1)}, s32[]{:S(2)}) async-start(s8[6635520]{0:T(1024)(128)(4,1)} %bitcast.65), calls=%async_computation.5 | async-start | bytes 4882432
  142.5 10.5 %all-to-all-start = ((f32[8,4,288]{2,1,0:T(4,128)}), f32[8,4,288]{2,1,0:T(4,128)S(1)}, u32[]{:S(2)}, u32[]{:S(2)}) async-start(f32[8,4,288]{2,1,0:T(4,128)} %fusion.9), calls=%async_computation | async-start | bytes 98304 | tf_op jit(solution)/shard_map/all_to_all | solution.py:96
  146.1 65.5 %all-reduce.5.cloned.1.call-start = ((), (), s32[]{:S(2)}) async-start(), calls=%async_computation.4 | async-start | bytes 1474560 | tf_op jit(solution)/shard_map/psum | solution.py:128
  173.6 4.1 %slice-start.1 = ((s8[6635520]{0:T(1024)(128)(4,1)}), s8[4194304]{0:T(1024)(128)(4,1)S(1)}, s32[]{:S(2)}) async-start(s8[6635520]{0:T(1024)(128)(4,1)} %bitcast.65), calls=%async_computation.6 | async-start | bytes 8388608
  177.8 2.0 copy-start.2
  218.3 12.1 %all-to-all-start.2 = ((bf16[8,2,576]{2,1,0:T(2,128)(2,1)}), bf16[8,2,576]{2,1,0:T(2,128)(2,1)S(1)}, u32[]{:S(2)}, u32[]{:S(2)}) async-start(bf16[8,2,576]{2,1,0:T(2,128)(2,1)} %copy.53), calls=%async_computation.2 | async-start | bytes 40960 | tf_op jit(solution)/shard_map/all_to_all | solution.py:132
Sparse Core Ops, SparseCore 0:
  73.2 67.1 all-reduce.2
  179.9 31.7 all-reduce.4
where the time goes:
time: 239 us; the launch traced here: 238 us
  waiting for transfers between devices  92.3 us (39%)
  blocking collectives  91.1 us (38%)
  between operations  14.3 us (6%)
  matrix products  13.6 us (6%)
  local copies, waits for them, and re-layouts  10.8 us (5%)
  starting transfers between devices  9.26 us (4%)
  other arithmetic  6.77 us (3%)
    psum x1, waiting for transfers between devices, per_device(): merged_sum, merged_acc = lax.psum((dense_sum, dense_acc), 'seq')  48.6 us
    all_gather x1, blocking collectives, per_device(): all_queries = lax.all_gather(new_query, 'seq', axis=0, tiled=True)  32.6 us
    psum x1, waiting for transfers between devices, per_device(): summed = lax.psum(stacked, 'tensor')  31.8 us
    pmax x1, blocking collectives, per_device(): global_top = lax.pmax(dense_top, 'seq')  21.5 us
    psum x1, blocking collectives, per_device(): merged_sum, merged_acc = lax.psum((dense_sum, dense_acc), 'seq')  17.6 us
    psum x1, blocking collectives, per_device(): attn_full = lax.psum(home_part, 'tensor')  10.5 us
    all_to_all x1, blocking collectives, per_device(): rows = lax.all_to_all(send, 'seq', split_axis=0, concat_axis=0, tiled=True)  8.97 us
    all_to_all x1, waiting for transfers between devices, per_device(): lax.all_to_all(expert_out.astype(jnp.bfloat16), 'seq', split_axis=0, conc...  5.93 us
  transfers between devices with their start and end apart: 4, of which 4 were waited for; matrix products, arithmetic and copies ran while one was open for 1% of the time, Pallas kernels for 0%

commit v1 on v0

--- a/solution.py
+++ b/solution.py
@@ -1,8 +1,11 @@
+import functools
 import math
 
 import jax
 import jax.numpy as jnp
 from jax import lax
+from jax.experimental import pallas as pl
+from jax.experimental.pallas import tpu as pltpu
 from jax.sharding import PartitionSpec as P
 
 HEAD_DIM = 64
@@ -140,6 +143,574 @@
     )
     return (attn_out, mixture_expert_partial.astype(jnp.bfloat16))
 
+LANES = 128
+MESH = pl.DeviceIdType.MESH
+HIGH = lax.Precision.HIGHEST
+f32 = jnp.float32
+bf16 = jnp.bfloat16
+
+
+def iota(shape, dim):
+    return lax.broadcasted_iota(jnp.int32, shape, dim)
+
+
+def dot(a, b, precision=None):
+    return jnp.dot(a, b, preferred_element_type=f32, precision=precision)
+
+
+def packed(x, strips):
+    gap = strips * LANES - x.shape[1]
+    if gap:
+        x = jnp.concatenate([x, jnp.zeros((x.shape[0], gap), x.dtype)], axis=1)
+    return [x[:, j * LANES : (j + 1) * LANES] for j in range(strips)]
+
+
+def layer_kernel(
+    n_seq,
+    n_tensor,
+    owner_ref,
+    fill_ref,
+    routes_ref,
+    rw_ref,
+    q_ref,
+    kn_ref,
+    vn_ref,
+    stream_ref,
+    gain_ref,
+    kc_hbm,
+    vc_hbm,
+    ow_hbm,
+    wg_hbm,
+    wu_hbm,
+    wd_hbm,
+    attn_ref,
+    moe_ref,
+    kc,
+    vc,
+    ow,
+    wg,
+    wu,
+    wd,
+    qbuf,
+    ebuf,
+    bbuf,
+    psend,
+    precv,
+    ssq,
+    gsend,
+    grecv,
+    hid,
+    osend,
+    orecv,
+    lsem,
+    qs,
+    qr,
+    es,
+    er,
+    bs,
+    br,
+    ps,
+    pr,
+    ss,
+    sr,
+    gs,
+    gr,
+    hs,
+    hr,
+    os_,
+    or_,
+):
+    s = lax.axis_index("seq")
+    t = lax.axis_index("tensor")
+    req, width = q_ref.shape
+    requests = req * n_seq
+    pages, slots, _ = kc.shape
+    heads = width // HEAD_DIM
+    strips = -(-width // LANES)
+    cols = ow.shape[1]
+    ff = wg_hbm.shape[2]
+    chunk = hid.shape[2]
+    rows = n_seq * CAP
+    hp = 16
+
+    loads = [
+        pltpu.make_async_copy(a, b, lsem.at[i])
+        for i, (a, b) in enumerate(
+            [
+                (kc_hbm, kc),
+                (vc_hbm, vc),
+                (ow_hbm, ow),
+                (wg_hbm.at[0], wg.at[:, 0:ff]),
+                (wu_hbm.at[0], wu.at[:, 0:ff]),
+                (wd_hbm.at[0], wd.at[0:ff, :]),
+            ]
+        )
+    ]
+    for load in loads:
+        load.start()
+
+    barrier = pltpu.get_barrier_semaphore()
+    total_devices = n_seq * n_tensor
+    me = s * n_tensor + t
+
+    def greet(i, carry):
+        other = lax.rem(me + i, total_devices)
+        pl.semaphore_signal(
+            barrier,
+            inc=1,
+            device_id=(other // n_tensor, lax.rem(other, n_tensor)),
+            device_id_type=MESH,
+        )
+        return carry
+
+    lax.fori_loop(1, total_devices, greet, 0)
+
+    def seq_copy(src, dst, send, recv, k, slot):
+        peer = lax.rem(s + k, n_seq)
+        return pltpu.make_async_remote_copy(
+            src_ref=src,
+            dst_ref=dst,
+            send_sem=send.at[k],
+            recv_sem=recv.at[slot],
+            device_id=(peer, t),
+            device_id_type=MESH,
+        )
+
+    def gather_start(buf, send, recv):
+        for k in range(1, n_seq):
+            seq_copy(buf.at[s], buf.at[s], send, recv, k, s).start()
+
+    def gather_wait(buf, send, recv):
+        for k in range(1, n_seq):
+            src = lax.rem(s + k, n_seq)
+            seq_copy(buf.at[src], buf.at[src], send, recv, k, src).wait_recv()
+
+    def gather_sent(buf, send, recv):
+        for k in range(1, n_seq):
+            seq_copy(buf.at[s], buf.at[s], send, recv, k, s).wait_send()
+
+    q = q_ref[...].astype(f32)
+    lane_row = iota((1, LANES), 1)
+    route_rows = []
+    for i in range(2):
+        row = jnp.zeros((1, LANES), f32)
+        for r in range(req):
+            value = jnp.full((1, LANES), routes_ref[r, i], jnp.int32).astype(f32)
+            row = jnp.where(lane_row == s * req + r, value, row)
+        route_rows.append(row)
+    rest = qbuf.shape[1] - strips * req - 2
+    qbuf[s] = jnp.concatenate(
+        packed(q, strips) + route_rows + [jnp.zeros((rest, LANES), f32)], axis=0
+    ).astype(bf16)
+
+    stream = stream_ref[...].astype(f32)
+    part = stream[:, 0:width]
+    gain = gain_ref[:, 0:width]
+    for i in range(1, n_tensor):
+        here = t == i
+        part = jnp.where(here, stream[:, i * width : (i + 1) * width], part)
+        gain = jnp.where(here, gain_ref[:, i * width : (i + 1) * width], gain)
+    vn = vn_ref[...].astype(f32)
+    rest = ebuf.shape[1] - 2 * strips * req
+    ebuf[s] = jnp.concatenate(
+        packed(part, strips) + packed(vn, strips) + [jnp.zeros((rest, LANES), f32)], axis=0
+    ).astype(bf16)
+
+    pl.semaphore_wait(barrier, total_devices - 1)
+    gather_start(qbuf, qs, qr)
+    gather_start(ebuf, es, er)
+
+    wg[:, ff:] = jnp.zeros((wg.shape[0], wg.shape[1] - ff), bf16)
+    wu[:, ff:] = jnp.zeros((wu.shape[0], wu.shape[1] - ff), bf16)
+    wd[ff:, :] = jnp.zeros((wd.shape[0] - ff, wd.shape[1]), bf16)
+
+    head_of = iota((width, LANES), 0) - HEAD_DIM * (iota((width, LANES), 1) - 16)
+    to_own = ((head_of >= 0) & (head_of < HEAD_DIM)).astype(f32)
+    from_head = iota((LANES, width), 1) - HEAD_DIM * iota((LANES, width), 0)
+    spread = ((from_head >= 0) & (from_head < HEAD_DIM)).astype(f32)
+    product = jnp.concatenate(
+        [q * kn_ref[...].astype(f32), jnp.zeros((8 - req, width), f32)], axis=0
+    )
+    own_row = dot(product, to_own, HIGH)[0:req] * (1.0 / math.sqrt(HEAD_DIM))
+
+    ph = pages * hp
+    sub = iota((ph, 1), 0)
+    page_row = sub >> 4
+    head_row = sub & 15
+    target = jnp.zeros((ph, 1), jnp.int32)
+    high = jnp.zeros((ph, 1), jnp.int32)
+    for p in range(pages):
+        owner = owner_ref[s * pages + p]
+        home = lax.div(owner, req)
+        target = jnp.where(
+            page_row == p, home * qbuf.shape[1] + (owner - home * req), target
+        )
+        high = jnp.where(page_row == p, p * slots + fill_ref[p], high)
+    lane = iota((ph, pages * slots), 1)
+    valid = (lane >= page_row * slots) & (lane < high)
+    channel = iota((ph, width), 1) - HEAD_DIM * head_row
+    head_mask = ((channel >= 0) & (channel < HEAD_DIM)).astype(f32)
+    qlane = iota((ph, n_seq * qbuf.shape[1]), 1)
+    picks = [(qlane == target + req * j).astype(bf16) for j in range(strips)]
+
+    all_pages = pages * n_seq
+    sub_r = iota((requests, LANES), 0)
+    lane_r = iota((requests, LANES), 1)
+    hot_pr = jnp.zeros((requests, LANES), f32)
+    hot_rp = jnp.zeros((requests, LANES), f32)
+    for p in range(all_pages):
+        owner = owner_ref[p]
+        hot_pr = jnp.where((sub_r == p) & (lane_r == owner), 1.0, hot_pr)
+        hot_rp = jnp.where((sub_r == owner) & (lane_r == p), 1.0, hot_rp)
+    hot_pr = hot_pr[:, 0:requests]
+    hot_rp = hot_rp[:, 0:all_pages]
+
+    loads[0].wait()
+    gather_wait(qbuf, qs, qr)
+    queries = qbuf[...].reshape(n_seq * qbuf.shape[1], LANES)
+    page_q = jnp.concatenate([dot(pick, queries) for pick in picks], axis=1)[:, 0:width]
+    page_q = (page_q * head_mask).astype(bf16)
+    keys = kc[...].reshape(pages * slots, width)
+    scores = lax.dot_general(
+        page_q, keys, (((1,), (1,)), ((), ())), preferred_element_type=f32
+    ) * (1.0 / math.sqrt(HEAD_DIM))
+    scores = jnp.where(valid, scores, low_value)
+    page_top = jnp.max(scores, axis=1, keepdims=True)
+    weights = jnp.exp(scores - page_top)
+    page_sum = jnp.sum(weights, axis=1, keepdims=True)
+    loads[1].wait()
+    values = vc[...].reshape(pages * slots, width)
+    page_acc = dot(weights.astype(bf16), values) * (head_mask * (1.0 / page_sum))
+    page_acc = jnp.sum(page_acc.reshape(pages, hp, width), axis=1)
+    level = page_top + jnp.log(page_sum)
+    level = jnp.where(iota((ph, LANES), 1) == head_row, level, 0.0)
+    level = jnp.sum(level.reshape(pages, hp, LANES), axis=1)
+    bbuf[s] = jnp.concatenate(packed(page_acc, strips) + [level + own_row], axis=0)
+    gather_start(bbuf, bs, br)
+
+    routed = qbuf[0, 16:32, :].astype(f32)
+    for i in range(1, n_seq):
+        routed = routed + qbuf[i, 16:32, :].astype(f32)
+    first = strips * req - 16
+    expert = jnp.full((1, LANES), s, jnp.int32).astype(f32)
+    chosen = jnp.where(
+        (routed[first : first + 1] == expert) | (routed[first + 1 : first + 2] == expert),
+        1.0,
+        0.0,
+    )
+    lane_1 = iota((1, LANES), 1)
+    chosen = jnp.where(lane_1 < requests, chosen, 0.0)
+    before_a = iota((LANES, LANES), 0)
+    before_b = iota((LANES, LANES), 1)
+    before = ((before_a < before_b) & ((before_a >> 2) == (before_b >> 2))).astype(bf16)
+    rank = dot(jnp.broadcast_to(chosen, (16, LANES)).astype(bf16), before)
+    slot_row = iota((rows, LANES), 0)
+    slot_lane = iota((rows, LANES), 1)
+    place = jnp.where(
+        ((slot_lane >> 2) == (slot_row >> 1))
+        & (rank == (slot_row & 1).astype(f32)),
+        jnp.broadcast_to(chosen, (rows, LANES)),
+        0.0,
+    )[:, 0:requests].astype(bf16)
+
+    home_row = iota((8, requests), 0)
+    at_home = ((iota((8, requests), 1) == home_row + s * req) & (home_row < req)).astype(bf16)
+
+    gather_wait(ebuf, es, er)
+
+    def unpacked(buf, offset, kind):
+        return jnp.concatenate(
+            [
+                jnp.concatenate(
+                    [
+                        buf[i].astype(f32)[offset + j * req : offset + (j + 1) * req]
+                        for i in range(n_seq)
+                    ],
+                    axis=0,
+                )
+                for j in range(strips)
+            ],
+            axis=1,
+        )[:, 0:width].astype(kind)
+
+    stream_rows = dot(place, unpacked(ebuf, 0, bf16))
+    new_values = unpacked(ebuf, strips * req, f32)
+
+    gather_wait(bbuf, bs, br)
+    levels = jnp.concatenate([bbuf[i, strips * req :, :] for i in range(n_seq)], axis=0)
+    own = jnp.concatenate([levels[:, 16:], levels[:, 0:16]], axis=1)
+    top = own
+    for p in range(all_pages):
+        top = jnp.maximum(top, jnp.where(sub_r == owner_ref[p], levels[p : p + 1], low_value))
+    factor = jnp.exp(levels - dot(hot_pr, top, HIGH))
+    own_factor = jnp.exp(own - top)
+    wide = dot(jnp.concatenate([factor, own_factor], axis=0), spread, HIGH)
+    page_wide, own_wide = wide[0:all_pages], wide[all_pages:]
+    acc = dot(hot_rp, page_wide * unpacked(bbuf, 0, f32), HIGH) + own_wide * new_values
+    total = 1.0 / (dot(hot_rp, factor, HIGH) + own_factor)
+    attended = (acc * dot(total, spread, HIGH)).astype(bf16)
+
+    loads[2].wait()
+    projected = dot(attended, ow[...])
+    psend[...] = jnp.concatenate(
+        [projected, jnp.zeros((requests, psend.shape[1] - cols), f32)], axis=1
+    ).astype(bf16)
+    ratio = n_seq // n_tensor
+    column = s // ratio
+    pslot = lax.rem(s, ratio) * n_tensor + t
+
+    def part_copy(k):
+        return pltpu.make_async_remote_copy(
+            src_ref=psend,
+            dst_ref=precv.at[pslot],
+            send_sem=ps.at[k],
+            recv_sem=pr.at[pslot],
+            device_id=(lax.rem(s + k, n_seq), column),
+            device_id_type=MESH,
+        )
+
+    def self_part():
+        return pltpu.make_async_copy(psend, precv.at[pslot], pr.at[pslot])
+
+    for k in range(1, n_seq):
+        part_copy(k).start()
+
+    @pl.when(column != t)
+    def _():
+        part_copy(0).start()
+
+    @pl.when(column == t)
+    def _():
+        self_part().start()
+
+    halves = []
+    for half in range(ratio):
+        piece = None
+        for i in range(n_tensor):
+            j = half * n_tensor + i
+            pltpu.make_async_copy(psend, precv.at[j], pr.at[j]).wait()
+            term = precv[j].astype(f32)
+            piece = term if piece is None else piece + term
+        halves.append(piece[:, 0:cols])
+    attn = jnp.concatenate(halves, axis=1).astype(bf16)
+
+    resid = stream_rows + dot(place, attn)
+    ssq[0] = jnp.broadcast_to(jnp.sum(resid * resid, axis=1, keepdims=True), (rows, LANES))
+    x = (resid * gain).astype(bf16)
+
+    low = lax.rem(t, 2)
+    partners = [t, t + 1 - 2 * low, lax.rem(t + 2, 4), 3 - t]
+
+    def tensor_copy(src, dst, send, recv, k, slot):
+        return pltpu.make_async_remote_copy(
+            src_ref=src,
+            dst_ref=dst,
+            send_sem=send.at[k],
+            recv_sem=recv.at[slot],
+            device_id=(s, partners[k]),
+            device_id_type=MESH,
+        )
+
+    ssq_copies = [None] + [
+        tensor_copy(ssq.at[0], ssq.at[k], ss, sr, k, k) for k in range(1, n_tensor)
+    ]
+    gate_copies = [None] + [
+        tensor_copy(gsend.at[k], grecv.at[k], gs, gr, k, k) for k in range(1, n_tensor)
+    ]
+    for k in range(1, n_tensor):
+        ssq_copies[k].start()
+    loads[3].wait()
+    loads[4].wait()
+    for k in (2, 3, 1, 0):
+        span = pl.ds(pl.multiple_of(partners[k] * chunk, LANES), chunk)
+        gate = dot(x, wg[:, span])
+        up = dot(x, wu[:, span])
+        if k:
+            gsend[k, 0] = gate.astype(bf16)
+            gsend[k, 1] = up.astype(bf16)
+            gate_copies[k].start()
+
+    attn_ref[...] = dot(at_home, attn)[0:req].astype(bf16)
+    mean = ssq[0]
+    for k in (1, 2, 3):
+        ssq_copies[k].wait_recv()
+        mean = mean + ssq[k]
+    root = lax.rsqrt(mean[:, 0:1] * (1.0 / (width * n_tensor)) + eps)
+    for k in (1, 2, 3):
+        gate_copies[k].wait_recv()
+        gate = gate + grecv[k, 0].astype(f32)
+        up = up + grecv[k, 1].astype(f32)
+    gate = gate * root
+    up = up * root
+    hid[0] = (gate / (1.0 + jnp.exp(-gate)) * up).astype(bf16)
+    hid_copies = [None] + [
+        tensor_copy(hid.at[0], hid.at[k], hs, hr, k, k) for k in range(1, n_tensor)
+    ]
+    for k in (2, 3, 1):
+        hid_copies[k].start()
+
+    wsub = iota((8 * strips, LANES), 0)
+    wlane = iota((8 * strips, LANES), 1) - CAP * (wsub >> 3)
+    mix = jnp.zeros((8 * strips, LANES), f32)
+    for r in range(req):
+        for i in range(2):
+            e = routes_ref[r, i]
+            taken = jnp.int32(0)
+            for r2 in range(r):
+                for i2 in range(2):
+                    taken = taken + (routes_ref[r2, i2] == e).astype(jnp.int32)
+            mix = jnp.where(
+                ((wsub & 7) == r) & (wlane == e * 16 + taken), rw_ref[r, i], mix
+            )
+
+    loads[5].wait()
+    out = None
+    for k in (0, 1, 2, 3):
+        if k:
+            hid_copies[k].wait_recv()
+        span = pl.ds(pl.multiple_of(partners[k] * chunk, LANES), chunk)
+        term = dot(hid[k], wd[span, :])
+        out = term if out is None else out + term
+
+    tiles = packed(out, strips)
+    fill = jnp.zeros((16 - CAP * strips, LANES), f32)
+    for d in range(n_seq):
+        osend[d] = jnp.concatenate(
+            [tile[CAP * d : CAP * (d + 1)] for tile in tiles] + [fill], axis=0
+        ).astype(bf16)
+    for k in range(1, n_seq):
+        peer = lax.rem(s + k, n_seq)
+        seq_copy(osend.at[peer], orecv.at[s], os_, or_, k, s).start()
+    orecv[s] = osend[s]
+    for k in range(1, n_seq):
+        peer = lax.rem(s + k, n_seq)
+        seq_copy(osend.at[peer], orecv.at[peer], os_, or_, k, peer).wait_recv()
+    returned = orecv[...].astype(f32).reshape(n_seq * 16, LANES)
+    mixed = dot(mix, returned, HIGH)
+    moe = jnp.concatenate([mixed[8 * j : 8 * j + req] for j in range(strips)], axis=1)
+    moe_ref[...] = moe[:, 0:width].astype(bf16)
+
+    gather_sent(qbuf, qs, qr)
+    gather_sent(ebuf, es, er)
+    gather_sent(bbuf, bs, br)
+    for k in range(1, n_seq):
+        part_copy(k).wait_send()
+
+    @pl.when(column != t)
+    def _():
+        part_copy(0).wait_send()
+
+    for k in range(1, n_tensor):
+        ssq_copies[k].wait_send()
+        gate_copies[k].wait_send()
+        hid_copies[k].wait_send()
+    for k in range(1, n_seq):
+        peer = lax.rem(s + k, n_seq)
+        seq_copy(osend.at[peer], orecv.at[s], os_, or_, k, s).wait_send()
+
+
+def one_kernel(n_seq, n_tensor, *args):
+    (
+        stream,
+        new_query,
+        k_new,
+        v_new,
+        k_cache,
+        v_cache,
+        page_owner,
+        page_fill,
+        out_weight,
+        norm_gain,
+        routes,
+        route_weight,
+        w_gate,
+        w_up,
+        w_down,
+    ) = args
+    req, width = new_query.shape
+    ff = w_gate.shape[2]
+    cols = out_weight.shape[1]
+    requests = req * n_seq
+    strips = -(-width // LANES)
+    chunk = -(-ff // (n_tensor * LANES)) * LANES
+    rows = n_seq * CAP
+    smem = pl.BlockSpec(memory_space=pltpu.SMEM)
+    vmem = pl.BlockSpec(memory_space=pltpu.VMEM)
+    hbm = pl.BlockSpec(memory_space=pl.ANY)
+    dma = pltpu.SemaphoreType.DMA
+    out = jax.ShapeDtypeStruct((req, width), bf16)
+    return pl.pallas_call(
+        functools.partial(layer_kernel, n_seq, n_tensor),
+        out_shape=(out, out),
+        in_specs=[smem] * 4 + [vmem] * 5 + [hbm] * 6,
+        out_specs=(vmem, vmem),
+        scratch_shapes=[
+            pltpu.VMEM(k_cache.shape, bf16),
+            pltpu.VMEM(v_cache.shape, bf16),
+            pltpu.VMEM(out_weight.shape, bf16),
+            pltpu.VMEM((width, chunk * n_tensor), bf16),
+            pltpu.VMEM((width, chunk * n_tensor), bf16),
+            pltpu.VMEM((chunk * n_tensor, width), bf16),
+            pltpu.VMEM((n_seq, 32, LANES), bf16),
+            pltpu.VMEM((n_seq, 48, LANES), bf16),
+            pltpu.VMEM((n_seq, 24, LANES), f32),
+            pltpu.VMEM((requests, -(-cols // LANES) * LANES), bf16),
+            pltpu.VMEM((n_seq, requests, -(-cols // LANES) * LANES), bf16),
+            pltpu.VMEM((n_tensor, rows, LANES), f32),
+            pltpu.VMEM((n_tensor, 2, rows, chunk), bf16),
+            pltpu.VMEM((n_tensor, 2, rows, chunk), bf16),
+            pltpu.VMEM((n_tensor, rows, chunk), bf16),
+            pltpu.VMEM((n_seq, 16, LANES), bf16),
+            pltpu.VMEM((n_seq, 16, LANES), bf16),
+            dma((6,)),
+        ]
+        + [dma((n_seq,))] * 8
+        + [dma((n_tensor,))] * 6
+        + [dma((n_seq,))] * 2,
+        compiler_params=pltpu.CompilerParams(
+            collective_id=0, has_side_effects=True, vmem_limit_bytes=56 * 1024 * 1024
+        ),
+        name="layer",
+    )(
+        page_owner,
+        page_fill,
+        routes,
+        route_weight,
+        new_query,
+        k_new,
+        v_new,
+        stream,
+        norm_gain.reshape(1, -1),
+        k_cache,
+        v_cache,
+        out_weight,
+        w_gate,
+        w_up,
+        w_down,
+    )
+
+
+def fits_one_kernel(n_seq, n_tensor, args):
+    req, width = args[1].shape
+    pages = args[4].shape[0]
+    strips = -(-width // LANES)
+    return (
+        n_seq == EXPERTS
+        and n_tensor == 4
+        and req == 4
+        and pages == 4
+        and strips == 5
+        and width % HEAD_DIM == 0
+        and width // HEAD_DIM <= 16
+        and args[8].shape[1] * (n_seq // n_tensor) == width
+    )
+
+
+def either(n_seq, n_tensor, *args):
+    if fits_one_kernel(n_seq, n_tensor, args):
+        return one_kernel(n_seq, n_tensor, *args)
+    return per_device(*args)
+
 
 def solution(mesh):
     in_specs = (
@@ -161,5 +732,5 @@
     )
     out_specs = (P("seq", "tensor"), P("seq", "tensor"))
     return jax.shard_map(
-        per_device, mesh=mesh, in_specs=in_specs, out_specs=out_specs, check_vma=False
-    )
+        functools.partial(either, mesh.shape["seq"], mesh.shape["tensor"]), mesh=mesh, in_specs=in_specs, out_specs=out_specs, check_vma=False
+    )

time: 239 us -> 60.5 us (0.25)
  waiting for transfers between devices: 92.3 us -> 0 us
  blocking collectives: 91.1 us -> 0 us
  Pallas kernels: 0 us -> 40.5 us
  between operations: 14.3 us -> 0.64 us
  matrix products: 13.6 us -> 0 us
  starting transfers between devices: 9.26 us -> 0 us
  local copies, waits for them, and re-layouts: 10.8 us -> 18.8 us
  other arithmetic: 6.77 us -> 0 us
    psum x2 -> x0, waiting for transfers between devices: 80.4 us -> none  [the longest x1 48.6 us: per_device(): merged_sum, merged_acc = lax.psum((dense_sum, dense_acc), 'seq')]
    pallas_call x0 -> x1, Pallas kernels: none -> 40.5 us  [one_kernel(): pl.pallas_call(functools.partial(layer_kernel, n_seq, n_tensor), out_shap...]
    all_gather x1 -> x0, blocking collectives: 32.6 us -> none  [per_device(): all_queries = lax.all_gather(new_query, 'seq', axis=0, tiled=True)]
    psum x2 -> x0, blocking collectives: 28.1 us -> none  [the longest x1 17.6 us: per_device(): merged_sum, merged_acc = lax.psum((dense_sum, dense_acc), 'seq')]
    pmax x1 -> x0, blocking collectives: 21.5 us -> none  [per_device(): global_top = lax.pmax(dense_top, 'seq')]
    unnamed x13 -> x6, local copies, waits for them, and re-layouts: 3.27 us -> 17.5 us
    dot_general x10 -> x0, matrix products: 13.6 us -> none  [the longest x1 4.7 us: per_device(): down = jnp.dot(hidden, w_down[0], preferred_element_type=jnp.float32)]
    all_to_all x2 -> x0, waiting for transfers between devices: 11.8 us -> none  [the longest x1 5.93 us: per_device(): lax.all_to_all(expert_out.astype(jnp.bfloat16), 'seq', split_axis=0, conc...]
  transfers between devices with their start and end apart: 4 -> 0, of which waited for: 4 -> 0; matrix products, arithmetic and copies ran while one was open for 1% -> 0% of each run, Pallas kernels for 0% -> 0%
where the time goes in v1:
time: 60.5 us; the launch traced here: 59.9 us
  Pallas kernels  40.5 us (67%)
  local copies, waits for them, and re-layouts  18.8 us (31%)
  between operations  0.64 us (1%)
    pallas_call x1, Pallas kernels, one_kernel(): pl.pallas_call(functools.partial(layer_kernel, n_seq, n_tensor), out_shap...  40.5 us
    unnamed x6, local copies, waits for them, and re-layouts  17.5 us
    reshape x1, local copies, waits for them, and re-layouts, one_kernel(): norm_gain.reshape(1, -1)  1.31 us

profile of v1, /device:TPU:0, one launch (start us, length us, event | category | flops | bytes accessed | tf_op | source)
XLA Modules:
  0.0 59.9 jit_solution(13012912486294495651)
XLA Ops:
  0.6 1.3 %copy.17.routes_ref = s32[4,2]{1,0:T(4,128)} copy(s32[4,2]{0,1:T(2,128)} %param.25) | data formatting | bytes 64 | tf_op args[10]
  2.0 1.3 %copy.18.rw_ref = f32[4,2]{1,0:T(4,128)} copy(f32[4,2]{0,1:T(2,128)} %param.26) | data formatting | bytes 64 | tf_op args[11]
  3.3 1.3 %reshape.7.gain_ref = f32[1,2304]{1,0:T(1,128)} reshape(f32[2304]{0:T(1024)} %param.24) | data formatting | bytes 18432 | tf_op jit(solution)/shard_map/reshape | solution.py:683
  4.6 1.9 %copy.19.ow_hbm = bf16[576,288]{1,0:T(8,128)(2,1)} copy(bf16[576,288]{0,1:T(8,128)(2,1)} %param.23) | data formatting | bytes 663552 | tf_op args[8]
  6.5 10.3 %copy.20.wd_hbm = bf16[1,5760,576]{2,1,0:T(8,128)(2,1)} copy(bf16[1,5760,576]{1,2,0:T(8,128)(2,1)} %param.29) | data formatting | bytes 13271040 | tf_op args[14]
  16.8 40.5 %layer.1 = (bf16[4,576]{1,0:T(4,128)(2,1)}, bf16[4,576]{1,0:T(4,128)(2,1)}) custom-call(s32[32]{0:T(128)} %owner_ref.1, s32[4]{0:T(128)} %fill_ref.1, s32[4,2]{1,0:T(4,128)} %copy.17.routes_ref, f32[4,2]{1,0:T(4,128)} %copy.18.rw_ref, bf16[4,576]{1,0:T(4,128)(2,1)} %q_ref.1, bf16[4,576]{1,0:T(4,128)(2,1)} %kn_ref.1, bf16[4,576]{1,0:T(4,128)(2,1)} %vn_ref.1, ...), custom_call_target="tpu_custom_call" | custom-call | tf_op jit(solution)/shard_map/layer/pallas_call | solution.py:642
  57.3 1.3 %copy.23 = bf16[4,576]{1,0:T(4,128)(2,1)} copy(bf16[4,576]{1,0:T(4,128)(2,1)} %get-tuple-element.4) | data formatting | bytes 9216
  58.6 1.3 %copy.24 = bf16[4,576]{1,0:T(4,128)(2,1)} copy(bf16[4,576]{1,0:T(4,128)(2,1)} %get-tuple-element.5) | data formatting | bytes 9216

commit v2 on v1

--- a/solution.py
+++ b/solution.py
@@ -158,6 +158,10 @@
     return jnp.dot(a, b, preferred_element_type=f32, precision=precision)
 
 
+def dot_t(a, b):
+    return lax.dot_general(a, b, (((1,), (1,)), ((), ())), preferred_element_type=f32)
+
+
 def packed(x, strips):
     gap = strips * LANES - x.shape[1]
     if gap:
@@ -183,8 +187,7 @@
     wg_hbm,
     wu_hbm,
     wd_hbm,
-    attn_ref,
-    moe_ref,
+    out_ref,
     kc,
     vc,
     ow,
@@ -227,7 +230,7 @@
     pages, slots, _ = kc.shape
     heads = width // HEAD_DIM
     strips = -(-width // LANES)
-    cols = ow.shape[1]
+    cols = ow.shape[0]
     ff = wg_hbm.shape[2]
     chunk = hid.shape[2]
     rows = n_seq * CAP
@@ -242,7 +245,7 @@
                 (ow_hbm, ow),
                 (wg_hbm.at[0], wg.at[:, 0:ff]),
                 (wu_hbm.at[0], wu.at[:, 0:ff]),
-                (wd_hbm.at[0], wd.at[0:ff, :]),
+                (wd_hbm.at[0], wd.at[:, 0:ff]),
             ]
         )
     ]
@@ -295,7 +298,7 @@
     for i in range(2):
         row = jnp.zeros((1, LANES), f32)
         for r in range(req):
-            value = jnp.full((1, LANES), routes_ref[r, i], jnp.int32).astype(f32)
+            value = jnp.full((1, LANES), routes_ref[i, r], jnp.int32).astype(f32)
             row = jnp.where(lane_row == s * req + r, value, row)
         route_rows.append(row)
     rest = qbuf.shape[1] - strips * req - 2
@@ -305,11 +308,12 @@
 
     stream = stream_ref[...].astype(f32)
     part = stream[:, 0:width]
-    gain = gain_ref[:, 0:width]
+    gains = gain_ref[...].reshape(1, -1)
+    gain = gains[:, 0:width]
     for i in range(1, n_tensor):
         here = t == i
         part = jnp.where(here, stream[:, i * width : (i + 1) * width], part)
-        gain = jnp.where(here, gain_ref[:, i * width : (i + 1) * width], gain)
+        gain = jnp.where(here, gains[:, i * width : (i + 1) * width], gain)
     vn = vn_ref[...].astype(f32)
     rest = ebuf.shape[1] - 2 * strips * req
     ebuf[s] = jnp.concatenate(
@@ -322,7 +326,7 @@
 
     wg[:, ff:] = jnp.zeros((wg.shape[0], wg.shape[1] - ff), bf16)
     wu[:, ff:] = jnp.zeros((wu.shape[0], wu.shape[1] - ff), bf16)
-    wd[ff:, :] = jnp.zeros((wd.shape[0] - ff, wd.shape[1]), bf16)
+    wd[:, ff:] = jnp.zeros((wd.shape[0], wd.shape[1] - ff), bf16)
 
     head_of = iota((width, LANES), 0) - HEAD_DIM * (iota((width, LANES), 1) - 16)
     to_own = ((head_of >= 0) & (head_of < HEAD_DIM)).astype(f32)
@@ -451,7 +455,7 @@
     attended = (acc * dot(total, spread, HIGH)).astype(bf16)
 
     loads[2].wait()
-    projected = dot(attended, ow[...])
+    projected = dot_t(attended, ow[...])
     psend[...] = jnp.concatenate(
         [projected, jnp.zeros((requests, psend.shape[1] - cols), f32)], axis=1
     ).astype(bf16)
@@ -530,7 +534,7 @@
             gsend[k, 1] = up.astype(bf16)
             gate_copies[k].start()
 
-    attn_ref[...] = dot(at_home, attn)[0:req].astype(bf16)
+    out_ref[0] = dot(at_home, attn)[0:req].astype(bf16)
     mean = ssq[0]
     for k in (1, 2, 3):
         ssq_copies[k].wait_recv()
@@ -554,13 +558,13 @@
     mix = jnp.zeros((8 * strips, LANES), f32)
     for r in range(req):
         for i in range(2):
-            e = routes_ref[r, i]
+            e = routes_ref[i, r]
             taken = jnp.int32(0)
             for r2 in range(r):
                 for i2 in range(2):
-                    taken = taken + (routes_ref[r2, i2] == e).astype(jnp.int32)
+                    taken = taken + (routes_ref[i2, r2] == e).astype(jnp.int32)
             mix = jnp.where(
-                ((wsub & 7) == r) & (wlane == e * 16 + taken), rw_ref[r, i], mix
+                ((wsub & 7) == r) & (wlane == e * 16 + taken), rw_ref[i, r], mix
             )
 
     loads[5].wait()
@@ -569,7 +573,7 @@
         if k:
             hid_copies[k].wait_recv()
         span = pl.ds(pl.multiple_of(partners[k] * chunk, LANES), chunk)
-        term = dot(hid[k], wd[span, :])
+        term = dot_t(hid[k], wd[:, span])
         out = term if out is None else out + term
 
     tiles = packed(out, strips)
@@ -588,7 +592,7 @@
     returned = orecv[...].astype(f32).reshape(n_seq * 16, LANES)
     mixed = dot(mix, returned, HIGH)
     moe = jnp.concatenate([mixed[8 * j : 8 * j + req] for j in range(strips)], axis=1)
-    moe_ref[...] = moe[:, 0:width].astype(bf16)
+    out_ref[1] = moe[:, 0:width].astype(bf16)
 
     gather_sent(qbuf, qs, qr)
     gather_sent(ebuf, es, er)
@@ -638,19 +642,19 @@
     vmem = pl.BlockSpec(memory_space=pltpu.VMEM)
     hbm = pl.BlockSpec(memory_space=pl.ANY)
     dma = pltpu.SemaphoreType.DMA
-    out = jax.ShapeDtypeStruct((req, width), bf16)
-    return pl.pallas_call(
+    out = jax.ShapeDtypeStruct((2, req, width), bf16)
+    both = pl.pallas_call(
         functools.partial(layer_kernel, n_seq, n_tensor),
-        out_shape=(out, out),
+        out_shape=out,
         in_specs=[smem] * 4 + [vmem] * 5 + [hbm] * 6,
-        out_specs=(vmem, vmem),
+        out_specs=vmem,
         scratch_shapes=[
             pltpu.VMEM(k_cache.shape, bf16),
             pltpu.VMEM(v_cache.shape, bf16),
-            pltpu.VMEM(out_weight.shape, bf16),
+            pltpu.VMEM((cols, width), bf16),
             pltpu.VMEM((width, chunk * n_tensor), bf16),
             pltpu.VMEM((width, chunk * n_tensor), bf16),
-            pltpu.VMEM((chunk * n_tensor, width), bf16),
+            pltpu.VMEM((width, chunk * n_tensor), bf16),
             pltpu.VMEM((n_seq, 32, LANES), bf16),
             pltpu.VMEM((n_seq, 48, LANES), bf16),
             pltpu.VMEM((n_seq, 24, LANES), f32),
@@ -674,20 +678,21 @@
     )(
         page_owner,
         page_fill,
-        routes,
-        route_weight,
+        routes.T,
+        route_weight.T,
         new_query,
         k_new,
         v_new,
         stream,
-        norm_gain.reshape(1, -1),
+        norm_gain,
         k_cache,
         v_cache,
-        out_weight,
+        out_weight.T,
         w_gate,
         w_up,
-        w_down,
-    )
+        jnp.swapaxes(w_down, 1, 2),
+    )
+    return both[0], both[1]
 
 
 def fits_one_kernel(n_seq, n_tensor, args):

time: 60.5 us -> 42.9 us (0.71)
  local copies, waits for them, and re-layouts: 18.8 us -> 1.31 us
    unnamed x6 -> x0, local copies, waits for them, and re-layouts: 17.5 us -> none
    squeeze x0 -> x1, local copies, waits for them, and re-layouts: none -> 1.31 us  [one_kernel(): return (both[0], both[1])]
    reshape x1 -> x0, local copies, waits for them, and re-layouts: 1.31 us -> none  [one_kernel(): norm_gain.reshape(1, -1)]
where the time goes in v2:
time: 42.9 us; the launch traced here: 42.7 us
  Pallas kernels  40.7 us (95%)
  local copies, waits for them, and re-layouts  1.31 us (3%)
  between operations  0.64 us (1%)
    pallas_call x1, Pallas kernels, one_kernel(): pl.pallas_call(functools.partial(layer_kernel, n_seq, n_tensor), out_shap...  40.7 us
    squeeze x1, local copies, waits for them, and re-layouts, one_kernel(): return (both[0], both[1])  1.31 us

profile of v2, /device:TPU:0, one launch (start us, length us, event | category | flops | bytes accessed | tf_op | source)
XLA Modules:
  0.0 42.7 jit_solution(5209744283415032428)
XLA Ops:
  0.6 40.7 %layer.1 = bf16[2,4,576]{2,1,0:T(4,128)(2,1)} custom-call(s32[32]{0:T(128)} %owner_ref.1, s32[4]{0:T(128)} %fill_ref.1, s32[2,4]{1,0:T(2,128)} %bitcast.10, f32[2,4]{1,0:T(2,128)} %bitcast.11, bf16[4,576]{1,0:T(4,128)(2,1)} %q_ref.1, bf16[4,576]{1,0:T(4,128)(2,1)} %kn_ref.1, bf16[4,576]{1,0:T(4,128)(2,1)} %vn_ref.1, bf16[4,2304]{1,0:T(4,128)(2,1)} %stream_ref.1, ...), custom_call_target="tpu_custom_call" | custom-call | tf_op jit(solution)/shard_map/layer/pallas_call | solution.py:646
  41.4 1.3 %slice_bitcast_fusion = (bf16[4,576]{1,0:T(4,128)(2,1)}, bf16[4,576]{1,0:T(4,128)(2,1)}) fusion(bf16[2,4,576]{2,1,0:T(4,128)(2,1)} %layer.1), kind=kLoop, calls=%fused_computation | loop fusion | bytes 18432 | tf_op jit(solution)/shard_map/squeeze | solution.py:695
